TPU v7x, 256 devices: a whole 4x4x8 slice. The times are simulated.
256 devices in a mesh: dp: 8 (over z_hi, y), pipe: 4 (over x), tensor: 8 (over z_lo, core).
Axes of the slice: x: 4, y: 4, z: 8 (z_hi: 2, z_lo: 4; z = z_hi * 4 + z_lo), core: 2. Of those that a mesh axis runs over, the one named last changes fastest.
Arguments:
- emb: bfloat16 [25600, 12288], P('tensor', 'dp'), may hold values from -0.17140086 to 0.17140086
- final_hidden: bfloat16 [192, 12288], P(None, 'dp'), may hold values from -8 to 8
- section_inputs: bfloat16 [4, 192, 12288], P('pipe', None, 'dp'), may hold values from -6 to 6
- gains: float32 [4, 12288], P('pipe', 'dp'), may hold values from 0.1 to 1.9
- token_ids: int32 [192], replicated, may hold values from 0 to 25599
- targets: int32 [192], replicated, may hold values from 0 to 25599
Outputs:
- emb_grad: bfloat16 [25600, 12288], P('tensor', ('dp', 'pipe'))
All inputs are finite; a program needn't handle non-finite values.
Results may differ from a plain program's by a relative error of at most 0.0067.
Values may be sent and summed in bfloat16 or wider, within the bound.
A program may use at most 128 MiB of HBM per device.

v0:
```python
import jax
import jax.numpy as jnp
from jax import lax
from jax.sharding import PartitionSpec as P

eps = 1e-05


def combined_all(value, axis, join):
    pieces = jax.tree.map(lambda part: lax.all_gather(part, axis), value)
    head = jax.tree.map(lambda part: part[0], pieces)
    tail = jax.tree.map(lambda part: part[1:], pieces)
    running, _ = lax.scan(lambda running, slab: (join(running, slab), None), head, tail)
    return running


def passed_along(value, axis, steps):
    count = lax.axis_size(axis)
    leading, last = (max(0, -steps), min(count, count - steps))
    return lax.ppermute(value, axis, [(source, source + steps) for source in range(leading, last)])


def feature_sums(first, second):
    return lax.psum((first, second), "dp")


def merge_softmax(earlier, later):
    top = jnp.maximum(earlier[0], later[0])
    total = earlier[1] * jnp.exp(earlier[0] - top) + later[1] * jnp.exp(later[0] - top)
    return (top, total)


def input_rows(gradient, token_ids, offset, vocab_rows):
    local_ids = token_ids - offset
    inside = (local_ids >= 0) & (local_ids < vocab_rows)
    target_rows = jnp.where(inside, local_ids, vocab_rows)
    summed = jax.ops.segment_sum(gradient.astype(jnp.float32), target_rows, vocab_rows + 1)
    return summed[:vocab_rows].astype(jnp.bfloat16)


def make_grad(logits, top, total, targets, start):
    probs = jnp.exp(logits - top[:, None]) / total[:, None]
    vocab_index = lax.broadcasted_iota(jnp.int32, logits.shape, 1) + start
    onehot = (vocab_index == targets[:, None]).astype(jnp.float32)
    return (probs - onehot).astype(jnp.bfloat16)


def local(emb, final_hidden, section_inputs, gains, token_ids, targets):
    n_pipe = lax.axis_size("pipe")
    n_data = lax.axis_size("dp")
    vocab_rows = emb.shape[0]
    columns = emb.shape[1]
    width = columns * n_data
    tensor_pos = lax.axis_index("tensor")
    pipe_pos = lax.axis_index("pipe")
    offset = tensor_pos * vocab_rows
    partial_value = lax.dot_general(
        final_hidden, emb, (((1,), (1,)), ((), ())), preferred_element_type=jnp.float32
    )
    saved = section_inputs[0].astype(jnp.float32)
    moments = jnp.stack([jnp.sum(saved, axis=1), jnp.sum(saved * saved, axis=1)], axis=1)
    logits, moments = feature_sums(partial_value, moments)
    local_top = jnp.max(logits, axis=1)
    local_total = jnp.sum(jnp.exp(logits - local_top[:, None]), axis=1)
    top, total = combined_all((local_top, local_total), "tensor", merge_softmax)
    logit_grad = make_grad(logits, top, total, targets, offset)
    hidden_terms = jnp.dot(logit_grad, emb, preferred_element_type=jnp.float32)
    mean_x = moments[:, 0] / width
    rstd = lax.rsqrt(moments[:, 1] / width - mean_x * mean_x + eps)
    normed = (saved - mean_x[:, None]) * rstd[:, None]
    gradient = lax.psum(hidden_terms, "tensor").astype(jnp.bfloat16)
    gain = gains[0]
    for section in range(n_pipe):
        scaled = gradient.astype(jnp.float32) * gain[None, :]
        first_sum, second_sum = feature_sums(
            jnp.sum(scaled, axis=1), jnp.sum(scaled * normed, axis=1)
        )
        delta = rstd[:, None] * (
            scaled - first_sum[:, None] / width - normed * (second_sum[:, None] / width)
        )
        gradient = (gradient.astype(jnp.float32) + delta).astype(jnp.bfloat16)
        if section + 1 < n_pipe:
            gradient = passed_along(gradient, "pipe", -1)
    head_grad = lax.dot_general(
        logit_grad, final_hidden, (((0,), (0,)), ((), ())), preferred_element_type=jnp.float32
    ).astype(jnp.bfloat16)
    row_grad = input_rows(gradient, token_ids, offset, vocab_rows)
    term = jnp.where(pipe_pos == n_pipe - 1, head_grad.astype(jnp.float32), 0.0) + jnp.where(
        pipe_pos == 0, row_grad.astype(jnp.float32), 0.0
    )
    result = lax.psum_scatter(term.astype(jnp.bfloat16), "pipe", scatter_dimension=1, tiled=True)
    return result


def solution(mesh):
    placed = (P("tensor", "dp"), P(None, "dp"), P("pipe", None, "dp"), P("pipe", "dp"), P(), P())
    return jax.shard_map(
        local, mesh=mesh, in_specs=placed, out_specs=P("tensor", ("dp", "pipe")), check_vma=False
    )
```

profile of v0, /device:TPU:1, one launch (start us, length us, event | category | flops | bytes accessed | tf_op | source)
XLA Modules:
  0.0 544.3 jit_solution(1772460208171369617)
XLA Ops:
  6.5 0.0 copy-start
  6.5 0.0 all-reduce.10.cloned.1.call-start
  6.5 1.1 copy-done
  7.6 8.5 %fusion.47 = f32[192,3200]{1,0:T(8,128)} fusion(bf16[192,1536]{1,0:T(8,128)(2,1)S(1)} %copy-done, bf16[3200,1536]{1,0:T(8,128)(2,1)} %param.8), kind=kOutput, calls=%fused_computation.79 | convolution fusion | flops 1887436800 | bytes 12877824 | tf_op jit(solution)/shard_map/dot_general | solution.py:57
  16.2 0.0 all-reduce.10.cloned.1.call-update
  16.2 0.0 reduce-scatter.4.cloned.1.call-start
  16.2 0.6 copy-done.5
  16.8 0.6 dynamic-slice
  18.0 0.0 copy-done.1
  18.0 0.2 convert_reduce_fusion
  18.2 0.2 fusion.20
  18.4 31.7 %psum.79 = f32[192,2]{0,1:T(2,128)S(1)} all-reduce(f32[192,2]{0,1:T(2,128)S(1)} %pad_maximum_fusion), channel_id=1, replica_groups=mesh['dp'=8,'pipe'=4,'tensor'=8] {'dp'}, use_global_device_ids=true, to_apply=%region_8.9 | all-reduce | flops 384 | bytes 3072 | tf_op jit(solution)/shard_map/psum | solution.py:24
  50.1 112.4 %all-reduce.10.cloned.1.call-done = f32[192,3200]{1,0:T(8,128)} async-done(((f32[192,3200]{1,0:T(8,128)}), f32[192,3200]{1,0:T(8,128)}) %all-reduce.10.cloned.1.call-update) | async-done | bytes 2457616 | tf_op jit(solution)/shard_map/psum | solution.py:24
  162.4 1.9 reduce_max.9
  164.3 0.3 dynamic-update-slice
  164.6 2.2 exponential_reduce_fusion
  166.8 0.3 dynamic-update-slice.1
  167.1 22.7 %all-reduce.2 = (f32[1536]{0:T(1024)S(1)}, f32[1536]{0:T(1024)S(1)}) all-reduce(f32[1536]{0:T(1024)S(1)} %dynamic-update-slice, f32[1536]{0:T(1024)S(1)} %dynamic-update-slice.1), channel_id=2, replica_groups=mesh['dp'=8,'pipe'=4,'tensor'=8] {'tensor'}, use_global_device_ids=true, to_apply=%add | all-reduce | flops 3072 | bytes 24576
  189.8 0.1 slice.35
  189.8 0.1 slice.36
  189.9 0.1 reshape.35
  190.0 0.1 reshape.36
  190.1 0.3 while.12
  190.4 6.8 %fusion.46 = f32[192,1536]{1,0:T(8,128)S(1)} fusion(bf16[3200,1536]{1,0:T(8,128)(2,1)} %param.8, f32[192,3200]{1,0:T(8,128)} %all-reduce.10.cloned.1.call-done, s32[3200]{0:T(1024)S(1)} %iota_add_fusion, f32[192]{0:T(256)S(1)} %get-tuple-element.34, f32[192]{0:T(256)S(1)} %get-tuple-element.33, s32[192]{0:T(256)S(1)} %copy-done.4), kind=kOutput, calls=%fused_computation.78 | convolution fusion | flops 1891123200 | bytes 13482752 | tf_op jit(solution)/shard_map/dot_general | solution.py:67
  197.2 59.0 %all-reduce.11 = bf16[192,1536]{1,0:T(8,128)(2,1)S(1)} all-reduce(f32[192,1536]{1,0:T(8,128)S(1)} %fusion.46), channel_id=1, replica_groups=mesh['dp'=8,'pipe'=4,'tensor'=8] {'tensor'}, use_global_device_ids=true, to_apply=%region_5.0 | all-reduce | flops 294912 | bytes 1769472 | tf_op jit(solution)/shard_map/psum | solution.py:71
  256.2 0.4 fusion.15
  256.6 28.1 %all-reduce.6 = (f32[192]{0:T(256)S(1)}, f32[192]{0:T(256)S(1)}) all-reduce(f32[192]{0:T(256)S(1)} %get-tuple-element.36, f32[192]{0:T(256)S(1)} %get-tuple-element.35), channel_id=1, replica_groups=mesh['dp'=8,'pipe'=4,'tensor'=8] {'dp'}, use_global_device_ids=true, to_apply=%region_12.13 | all-reduce | flops 384 | bytes 3072 | tf_op jit(solution)/shard_map/psum | solution.py:24
  284.7 0.6 fusion.19
  285.3 1.3 collective-permute-start
  286.6 10.1 %collective-permute-done = bf16[192,1536]{1,0:T(8,128)(2,1)S(1)} collective-permute-done((bf16[192,1536]{1,0:T(8,128)(2,1)S(1)}, bf16[192,1536]{1,0:T(8,128)(2,1)S(1)}, u32[]{:S(2)}, u32[]{:S(2)}) %collective-permute-start) | collective-permute-done | bytes 589856 | tf_op jit(solution)/shard_map/ppermute | solution.py:20
  296.6 0.4 fusion.10
  297.0 20.3 %all-reduce.5 = (f32[192]{0:T(256)S(1)}, f32[192]{0:T(256)S(1)}) all-reduce(f32[192]{0:T(256)S(1)} %get-tuple-element.42, f32[192]{0:T(256)S(1)} %get-tuple-element.41), channel_id=1, replica_groups=mesh['dp'=8,'pipe'=4,'tensor'=8] {'dp'}, use_global_device_ids=true, to_apply=%region_16.17 | all-reduce | flops 384 | bytes 3072 | tf_op jit(solution)/shard_map/psum | solution.py:24
  317.4 0.6 fusion.33
  317.9 1.3 collective-permute-start.1
  319.2 9.3 %collective-permute-done.1 = bf16[192,1536]{1,0:T(8,128)(2,1)S(1)} collective-permute-done((bf16[192,1536]{1,0:T(8,128)(2,1)S(1)}, bf16[192,1536]{1,0:T(8,128)(2,1)S(1)}, u32[]{:S(2)}, u32[]{:S(2)}) %collective-permute-start.1) | collective-permute-done | bytes 589856 | tf_op jit(solution)/shard_map/ppermute | solution.py:20
  328.6 0.4 fusion.7
  329.0 21.8 %all-reduce.4 = (f32[192]{0:T(256)S(1)}, f32[192]{0:T(256)S(1)}) all-reduce(f32[192]{0:T(256)S(1)} %get-tuple-element.40, f32[192]{0:T(256)S(1)} %get-tuple-element.39), channel_id=1, replica_groups=mesh['dp'=8,'pipe'=4,'tensor'=8] {'dp'}, use_global_device_ids=true, to_apply=%region_20.21 | all-reduce | flops 384 | bytes 3072 | tf_op jit(solution)/shard_map/psum | solution.py:24
  350.7 0.6 fusion.35
  351.3 1.3 collective-permute-start.2
  352.7 9.6 %collective-permute-done.2 = bf16[192,1536]{1,0:T(8,128)(2,1)S(1)} collective-permute-done((bf16[192,1536]{1,0:T(8,128)(2,1)S(1)}, bf16[192,1536]{1,0:T(8,128)(2,1)S(1)}, u32[]{:S(2)}, u32[]{:S(2)}) %collective-permute-start.2) | collective-permute-done | bytes 589856 | tf_op jit(solution)/shard_map/ppermute | solution.py:20
  362.3 0.4 fusion.4
  362.6 20.7 %all-reduce.3 = (f32[192]{0:T(256)S(1)}, f32[192]{0:T(256)S(1)}) all-reduce(f32[192]{0:T(256)S(1)} %get-tuple-element.38, f32[192]{0:T(256)S(1)} %get-tuple-element.37), channel_id=1, replica_groups=mesh['dp'=8,'pipe'=4,'tensor'=8] {'dp'}, use_global_device_ids=true, to_apply=%region_24.25 | all-reduce | flops 384 | bytes 3072 | tf_op jit(solution)/shard_map/psum | solution.py:24
  383.4 10.9 %scatter_custom_fusion = f32[3201,1536]{1,0:T(8,128)} fusion(s32[192]{0:T(256)S(1)} %and_select_fusion, f32[]{:T(128)} %constant.39.clone.1, bf16[1,192,1536]{2,1,0:T(8,128)(2,1)S(1)} %copy-done.1, bf16[192,1536]{1,0:T(8,128)(2,1)S(1)} %collective-permute-done.2, f32[192]{0:T(256)S(1)} %broadcast_multiply_fusion, f32[192]{0:T(256)S(1)} %broadcast_multiply_fusion.1, ...), kind=kCustom, calls=%fused_computation.7 | custom fusion | flops 3833856 | bytes 20858884 | tf_op jit(solution)/shard_map/scatter-add | solution.py:37
  394.3 11.8 %add_convert_fusion = bf16[3200,1536]{1,0:T(8,128)(2,1)} fusion(bf16[192,1536]{1,0:T(8,128)(2,1)S(1)} %copy-done, f32[3201,1536]{1,0:T(8,128)} %scatter_custom_fusion, pred[]{:T(512)S(6)} %eq.17, pred[]{:T(512)S(6)} %eq.14, f32[192,3200]{1,0:T(8,128)} %all-reduce.10.cloned.1.call-done, s32[3200]{0:T(1024)S(1)} %iota_add_fusion, ...), kind=kOutput, calls=%fused_computation.5 | convolution fusion | flops 1925529600 | bytes 22723330 | tf_op jit(solution)/shard_map/dot_general | solution.py:84
  406.1 13.0 %copy.7 = bf16[3200,1536]{0,1:T(8,128)(2,1)} copy(bf16[3200,1536]{1,0:T(8,128)(2,1)} %add_convert_fusion) | data formatting | bytes 19660800
  419.1 0.0 reduce-scatter.4.cloned.1.call-update
  419.1 114.0 %reduce-scatter.4.cloned.1.call-done = bf16[384,3200]{1,0:T(8,128)(2,1)} async-done(((bf16[1536,3200]{1,0:T(8,128)(2,1)}), bf16[384,3200]{1,0:T(8,128)(2,1)}) %reduce-scatter.4.cloned.1.call-update) | async-done | bytes 2457616
  533.1 4.3 copy.8
  (38 shorter events, 0.3 us)
Async XLA Ops:
  6.5 1.1 copy-start
  6.5 155.9 %all-reduce.10.cloned.1.call-start = ((), (), s32[]{:S(2)}) async-start(), calls=%async_computation.1 | async-start | bytes 4915200 | tf_op jit(solution)/shard_map/psum | solution.py:24
  16.1 0.7 copy-start.5
  16.1 1.8 copy-start.2
  16.2 1.9 copy-start.1
  16.2 517.0 %reduce-scatter.4.cloned.1.call-start = ((), (), s32[]{:S(2)}) async-start(), calls=%async_computation.2 | async-start | bytes 12288000
  164.6 25.8 %copy-start.4 = (s32[192]{0:T(256)S(1)}, s32[192]{0:T(256)}, u32[]{:S(2)}) copy-start(s32[192]{0:T(256)} %param.13) | copy-start | bytes 2308
  285.3 11.3 %collective-permute-start = (bf16[192,1536]{1,0:T(8,128)(2,1)S(1)}, bf16[192,1536]{1,0:T(8,128)(2,1)S(1)}, u32[]{:S(2)}, u32[]{:S(2)}) collective-permute-start(bf16[192,1536]{1,0:T(8,128)(2,1)S(1)} %fusion.19), channel_id=1, source_target_pairs={{8,0},{16,8},{24,16},{9,1},{17,9},{25,17},{10,2},{18,10},{26,18},{... | collective-permute-start | bytes 1769480 | tf_op jit(solution)/shard_map/ppermute | solution.py:20
  317.9 10.6 %collective-permute-start.1 = (bf16[192,1536]{1,0:T(8,128)(2,1)S(1)}, bf16[192,1536]{1,0:T(8,128)(2,1)S(1)}, u32[]{:S(2)}, u32[]{:S(2)}) collective-permute-start(bf16[192,1536]{1,0:T(8,128)(2,1)S(1)} %fusion.33), channel_id=1, source_target_pairs={{8,0},{16,8},{24,16},{9,1},{17,9},{25,17},{10,2},{18,10},{26,18},{... | collective-permute-start | bytes 1769480 | tf_op jit(solution)/shard_map/ppermute | solution.py:20
  329.0 23.7 %copy-start.3 = (s32[192]{0:T(256)S(1)}, s32[192]{0:T(256)}, u32[]{:S(2)}) copy-start(s32[192]{0:T(256)} %param.12) | copy-start | bytes 2308
  351.3 10.9 %collective-permute-start.2 = (bf16[192,1536]{1,0:T(8,128)(2,1)S(1)}, bf16[192,1536]{1,0:T(8,128)(2,1)S(1)}, u32[]{:S(2)}, u32[]{:S(2)}) collective-permute-start(bf16[192,1536]{1,0:T(8,128)(2,1)S(1)} %fusion.35), channel_id=1, source_target_pairs={{8,0},{16,8},{24,16},{9,1},{17,9},{25,17},{10,2},{18,10},{26,18},{... | collective-permute-start | bytes 1769480 | tf_op jit(solution)/shard_map/ppermute | solution.py:20
Sparse Core Ops, SparseCore 0:
  16.3 146.0 all-reduce.9
  419.2 113.8 reduce-scatter.3
where the time goes:
time: 545 us; the launch traced here: 544 us
  waiting for transfers between devices  255 us (47%)
  blocking collectives  204 us (37%)
  matrix products  27.1 us (5%)
  local copies, waits for them, and re-layouts  20.4 us (4%)
  other arithmetic  18.9 us (3%)
  between operations  14.1 us (3%)
    psum x5, blocking collectives, feature_sums(): return lax.psum((first, second), 'dp')  123 us
    unnamed x3, waiting for transfers between devices  114 us
    psum x1, waiting for transfers between devices, feature_sums(): return lax.psum((first, second), 'dp')  112 us
    psum x1, blocking collectives, local(): gradient = lax.psum(hidden_terms, 'tensor').astype(jnp.bfloat16)  59 us
    ppermute x3, waiting for transfers between devices, passed_along(): lax.ppermute(value, axis, [(source, source + steps) for source in range(l...  29 us
    unnamed x1, blocking collectives  22.7 us
    unnamed x19, local copies, waits for them, and re-layouts  20.1 us
    dot_general x1, matrix products, local(): lax.dot_general(logit_grad, final_hidden, (((0,), (0,)), ((), ())), prefe...  11.8 us
  transfers between devices with their start and end apart: 5, of which 5 were waited for; matrix products, arithmetic and copies ran while one was open for 0% of the time, Pallas kernels for 0%

commit v1 on v0

v1 whole, which is shorter than its diff:
```python
import functools

import jax
import jax.numpy as jnp
from jax import lax
from jax.experimental import pallas as pl
from jax.experimental.pallas import tpu as pltpu
from jax.sharding import PartitionSpec as P

eps = 1e-05
f32 = jnp.float32
bf16 = jnp.bfloat16
MESH = pl.DeviceIdType.MESH
LOW = -3.0e38

T, V, C = 192, 3200, 1536
D = 12288
W = 896
Q = 384
B = 48
H = 96
R = 24
N_SEM = 128


def iota(shape, axis):
    return lax.broadcasted_iota(jnp.int32, shape, axis)


def pick_rows(rows, count):
    index = iota((count, 128), 0)
    out = jnp.zeros((count, 128), f32)
    for i, row in enumerate(rows):
        out = jnp.where(index == i, jnp.broadcast_to(row, (count, 128)), out)
    return out


def to_rows(cols, count):
    n = cols[0].shape[0]
    lane = iota((n, 128), 1)
    out = jnp.zeros((n, 128), f32)
    for i, col in enumerate(cols):
        out = jnp.where(lane == i, col, out)
    out = jnp.concatenate([out, jnp.zeros((128 - n, 128), f32)], axis=0)
    return out.T[:count]


def to_cols(tile):
    r = tile.shape[0]
    return jnp.concatenate([tile, jnp.zeros((128 - r, 128), f32)], axis=0).T


def kernel(
    emb, fh_h, x_h, gains_h, tgt_h, hd_out, g0_out,
    ew, ec, fh, xv, gv, tv, tcol, gb,
    lp, ly, zl_buf, zr_buf, pb,
    st, st2, sc,
    xt, xsl, xz, xs, gs, cs, rr, xhs,
    gt, gx, gt2, gy, gt3, gz, gram,
    G, cr, gh, zrs, ga, sm, smz, sm2, smxy, g0f, g0b, hd,
    lsem, ss, rs,
):
    d = lax.axis_index("dp")
    px = lax.axis_index("pipe")
    t = lax.axis_index("tensor")
    y, zh = d % 4, d // 4
    zl, c = t // 2, t % 2
    z = zh * 4 + zl

    def at(x_=None, y_=None, z_=None, c_=None):
        x_ = px if x_ is None else x_
        y_ = y if y_ is None else y_
        z_ = z if z_ is None else z_
        c_ = c if c_ is None else c_
        return ((z_ // 4) * 4 + y_, x_, (z_ % 4) * 2 + c_)

    def xy(i):
        return at(x_=(px + i // 4) % 4, y_=(y + i % 4) % 4)

    def zring(k):
        return at(z_=(z + k) % 8)

    def zline(k):
        return zh * 4 + (zl + k) % 4

    used = [0]

    def sems(n):
        used[0] += n
        assert used[0] <= N_SEM
        return used[0] - n

    def rc(src, dst, i, dev):
        return pltpu.make_async_remote_copy(
            src_ref=src, dst_ref=dst, send_sem=ss.at[i], recv_sem=rs.at[i],
            device_id=dev, device_id_type=MESH,
        )

    pending = []

    def send(cp):
        cp.start()
        pending.append(cp)
        return cp

    mult = pl.multiple_of
    my_tok = pl.ds(mult(c * H, 16), H)
    other_tok = pl.ds(mult((1 - c) * H, 16), H)

    loads = [
        pltpu.make_async_copy(x_h.at[0], xv, lsem.at[0]),
        pltpu.make_async_copy(gains_h, gv, lsem.at[1]),
        pltpu.make_async_copy(tgt_h, tv, lsem.at[2]),
        pltpu.make_async_copy(fh_h, fh, lsem.at[3]),
        pltpu.make_async_copy(emb.at[pl.ds(mult(px * 768, 128), W), :], ew, lsem.at[4]),
        pltpu.make_async_copy(emb.at[:, pl.ds(mult(px * Q, 128), Q)], ec, lsem.at[5]),
    ]
    for cp in loads:
        cp.start()
    bar = pltpu.get_barrier_semaphore()

    @pl.loop(1, 16)
    def _(i):
        pl.semaphore_signal(bar, inc=1, device_id=xy(i), device_id_type=MESH)

    for k in range(1, 8):
        pl.semaphore_signal(bar, inc=1, device_id=zring(k), device_id_type=MESH)
    for k in range(4):
        pl.semaphore_signal(bar, inc=1, device_id=at(z_=zline(k), c_=1 - c), device_id_type=MESH)

    loads[0].wait()
    xf = xv[my_tok, :].astype(f32)
    xt[...] = to_rows([jnp.sum(xf, axis=1, keepdims=True), jnp.sum(xf * xf, axis=1, keepdims=True)], 8)
    loads[1].wait()
    gb[...] = jnp.broadcast_to(gv[...], (8, C))
    loads[2].wait()
    tcol[...] = jnp.sum(
        jnp.where(iota((T, T), 0) == iota((T, T), 1), tv[...].astype(f32), 0.0), axis=1, keepdims=True
    ).astype(jnp.int32)

    loads[3].wait()
    loads[4].wait()

    @pl.loop(0, 7)
    def _(i):
        tile = pl.ds(mult(i * 128, 128), 128)
        lp[:, tile] = lax.dot_general(
            fh[...], ew[tile, :], (((1,), (1,)), ((), ())), preferred_element_type=f32
        )

    pl.semaphore_wait(bar, 26)

    sy = sems(3)
    ycp = []
    for k in (1, 3, 2):
        to = (y + k) % 4
        ycp.append(send(rc(lp.at[pl.ds(mult(to * B, 16), B), :], ly.at[k - 1], sy + k - 1, at(y_=to))))

    sx = sems(3)
    sg = sems(3)
    for k in range(1, 4):
        to = (px + k) % 4
        cols = pl.ds(mult(to * Q, 128), Q)
        send(rc(xv.at[my_tok, cols], xs.at[px], sx + k - 1, at(x_=to)))
        send(rc(gb.at[:, cols], gs.at[px], sg + k - 1, at(x_=to)))
    my_cols = pl.ds(mult(px * Q, 128), Q)
    xs[px] = xv[my_tok, my_cols]
    gs[px] = gb[:, my_cols]
    s1 = sems(16)
    xsl[px * 4 + y] = xt[...]

    @pl.loop(1, 16)
    def _(i):
        rc(xt, xsl.at[px * 4 + y], s1 + i, xy(i)).start()

    @pl.loop(1, 16)
    def _(i):
        slot = ((px - i // 4 + 4) % 4) * 4 + (y - i % 4 + 4) % 4
        rc(xt, xsl.at[slot], s1 + i, xy(i)).wait_recv()

    rows = []
    for s in range(4):
        tot = xsl[4 * s] + xsl[4 * s + 1] + xsl[4 * s + 2] + xsl[4 * s + 3]
        rows += [tot[0:1], tot[1:2]]
    xz[0] = pick_rows(rows, 8)
    s2 = sems(1)
    xzcp = send(rc(xz.at[0], xz.at[1], s2, zring(4)))

    for cp in ycp:
        cp.wait_recv()
    zl_buf[...] = lp[pl.ds(mult(y * B, 16), B), :] + ly[0] + ly[1] + ly[2]
    sz = sems(1)
    zcp = send(rc(zl_buf, zr_buf, sz, zring(4)))

    xzcp.wait_recv()
    tot = (xz[0] + xz[1]) * (1.0 / D)
    mu_rows, r_rows = [], []
    for s in range(4):
        mu = tot[2 * s : 2 * s + 1]
        mu_rows.append(mu)
        r_rows.append(lax.rsqrt(tot[2 * s + 1 : 2 * s + 2] - mu * mu + eps))
    rr[...] = pick_rows(r_rows, 8)
    cs[...] = to_cols(pick_rows(mu_rows + r_rows, 8))
    for k in range(1, 4):
        src = (px - k + 4) % 4
        rc(xv.at[my_tok, my_cols], xs.at[src], sx + k - 1, at(x_=src)).wait_recv()
        rc(gb.at[:, my_cols], gs.at[src], sg + k - 1, at(x_=src)).wait_recv()
    for s in range(4):
        xhs[s] = (xs[s].astype(f32) - cs[0:H, s : s + 1]) * cs[0:H, 4 + s : 5 + s]

    def gain(s):
        return gs[s][0:1, :]

    def rsum(v):
        return jnp.sum(v, axis=1, keepdims=True)

    cols = []
    for j in range(1, 4):
        q1 = jnp.ones((H, Q), f32)
        q2 = xhs[j]
        for s in range(j - 1, -1, -1):
            a1 = q1 * gain(s)
            a2 = q2 * gain(s)
            xh = xhs[s]
            cols += [rsum(a1), rsum(a1 * xh), rsum(a2), rsum(a2 * xh)]
            if s > 0:
                r_col = cs[0:H, 4 + s : 5 + s]
                q1 = q1 + r_col * a1
                q2 = q2 + r_col * a2
    gt[...] = to_rows(cols, 24)
    sgx = sems(3)
    gxcp = [send(rc(gt, gx.at[k - 1], sgx + k - 1, at(x_=(px + k) % 4))) for k in range(1, 4)]

    zcp.wait_recv()
    my_rows = pl.ds(mult(y * B, 16), B)
    lane = iota((B, W), 1)
    valid = lane >= jnp.where(px == 0, 0, 128)
    logits = jnp.where(valid, zl_buf[...] + zr_buf[...], LOW)
    m = jnp.max(logits, axis=1, keepdims=True)
    e = jnp.where(valid, jnp.exp(logits - m), 0.0)
    hit = (lane + (t * V + px * 768) == tcol[my_rows, :]) & valid
    tl = rsum(jnp.where(hit, logits, 0.0))
    pb[px, my_rows, :] = e.astype(bf16)
    st[0] = to_rows([m, rsum(e), tl], 8)

    def peer1(k):
        return at(x_=(px + k * c) % 4, y_=(y + k * (1 - c)) % 4)

    def peer2(k):
        return at(x_=(px + k * (1 - c)) % 4, y_=(y + k * c) % 4)

    def block(b, e_):
        bx = (px - b * c - e_ * (1 - c) + 4) % 4
        by = (y - b * (1 - c) - e_ * c + 4) % 4
        return bx, by

    def pref(b, e_):
        bx, by = block(b, e_)
        return pb.at[bx, pl.ds(mult(by * B, 16), B), :]

    a1 = sems(3)
    a2 = sems(12)
    sst = sems(8)
    for k in (1, 3, 2):
        send(rc(pref(0, 0), pref(0, 0), a1 + k - 1, peer1(k)))
    stcp = []
    for k in range(1, 8):
        stcp.append(send(rc(st.at[0], st.at[k], sst + k, at(z_=zline(k // 2), c_=(c + k % 2) % 2))))
    for k in (1, 3, 2):
        send(rc(pref(0, 0), pref(0, 0), a2 + k - 1, peer2(k)))

    for cp in gxcp:
        cp.wait_recv()
    gt2[...] = gt[...] + gx[0] + gx[1] + gx[2]
    sgy = sems(3)
    gycp = [send(rc(gt2, gy.at[k - 1], sgy + k - 1, at(y_=(y + k) % 4))) for k in range(1, 4)]

    for cp in stcp:
        cp.wait_recv()
    tiles = [st[k] for k in range(8)]
    top = functools.reduce(jnp.maximum, [a[0:1] for a in tiles])
    total = sum(a[1:2] * jnp.exp(a[0:1] - top) for a in tiles)
    hitsum = sum(a[2:3] for a in tiles)
    mine = px * 4 + y
    st2[mine] = pick_rows([top, total, hitsum, tiles[0][0:1]], 8)
    s3 = sems(16)

    @pl.loop(1, 16)
    def _(i):
        rc(st2.at[mine], st2.at[mine], s3 + i, xy(i)).start()

    for b in (1, 3, 2):
        rc(pref(0, 0), pref(b, 0), a1 + b - 1, peer1(b)).wait_recv()
        for k in (1, 3, 2):
            send(rc(pref(b, 0), pref(b, 0), a2 + 3 * b + k - 1, peer2(k)))

    for cp in gycp:
        cp.wait_recv()
    gt3[...] = gt2[...] + gy[0] + gy[1] + gy[2]
    sgz = sems(1)
    gzcp = send(rc(gt3, gz, sgz, zring(4)))

    @pl.loop(1, 16)
    def _(i):
        slot = ((px - i // 4 + 4) % 4) * 4 + (y - i % 4 + 4) % 4
        rc(st2.at[mine], st2.at[slot], s3 + i, xy(i)).wait_recv()

    rows = []
    for yy in range(4):
        tiles = [st2[4 * xx + yy] for xx in range(4)]
        top = functools.reduce(jnp.maximum, [a[0:1] for a in tiles])
        total = sum(a[1:2] * jnp.exp(a[0:1] - top) for a in tiles)
        inv = 1.0 / total
        rows += [jnp.exp(a[3:4] - top) * inv for a in tiles]
        rows += [jnp.exp(sum(a[2:3] for a in tiles) - top) * inv - 1.0]
        rows += [jnp.zeros((1, 128), f32)] * 3
    sc[...] = to_cols(pick_rows(rows, 32))

    def normalise(b, e_):
        bx, by = block(b, e_)
        blk = pl.ds(mult(by * B, 16), B)
        scale = rsum(jnp.where(iota((B, 128), 1) == by * 8 + bx, sc[0:B, :], 0.0))
        point = rsum(jnp.where(iota((B, 128), 1) == by * 8 + 4, sc[0:B, :], 0.0))
        hit = (lane + (t * V + bx * 768) == tcol[blk, :]) & (lane >= jnp.where(bx == 0, 0, 128))
        pb[bx, blk, :] = jnp.where(hit, point, pb[bx, blk, :].astype(f32) * scale).astype(bf16)

    for cp in pending:
        cp.wait_send()
    pending.clear()

    @pl.loop(0, 4)
    def _(b):
        normalise(b, 0)

    for b in (0, 1, 3, 2):
        for k in (1, 3, 2):
            rc(pref(0, 0), pref(b, k), a2 + 3 * b + k - 1, peer2(k)).wait_recv()
            normalise(b, k)

    loads[5].wait()
    G[...] = jnp.dot(pb[0], ec[0:W, :], preferred_element_type=f32)

    @pl.loop(1, 4)
    def _(i):
        G[...] += jnp.dot(pb[i], ec[pl.ds(mult(i * 768, 128), W), :], preferred_element_type=f32)

    sc0 = sems(1)
    corecp = send(rc(G.at[other_tok, :], cr, sc0, at(c_=1 - c)))
    gzcp.wait_recv()
    gram[...] = gt3[...] + gz[...]
    corecp.wait_recv()
    gh[...] = G[my_tok, :] + cr[...]
    szr = sems(3)
    zrcp = []
    for k in (1, 3, 2):
        to = (zl + k) % 4
        zrcp.append(send(rc(gh.at[pl.ds(mult(to * R, 8), R), :], zrs.at[k - 1], szr + k - 1, at(z_=zline(k)))))

    q = gh[...]
    cols = []
    for s in (3, 2, 1, 0):
        a = q * gain(s)
        cols += [rsum(a), rsum(a * xhs[s])]
        if s > 0:
            q = q + cs[0:H, 4 + s : 5 + s] * a
    sm[...] = to_rows(cols, 8)
    ssm = sems(8)
    smcp = [send(rc(sm, smz.at[k], ssm + k, zring(k))) for k in range(1, 8)]

    fcols = fh[:, my_cols]

    def head(lo, hi):
        @pl.loop(lo, hi)
        def _(i):
            xx = jnp.maximum(i - 1, 0) // 6
            loc = i - 6 * xx
            out = lax.dot_general(
                pb[xx, :, pl.ds(mult(loc * 128, 128), 128)], fcols,
                (((0,), (0,)), ((), ())), preferred_element_type=f32,
            )
            hd[pl.ds(mult(i * 128, 128), 128), :] = out.astype(bf16)

    head(0, 12)

    for cp in zrcp:
        cp.wait_recv()
    mine24 = gh[pl.ds(mult(zl * R, 8), R), :] + zrs[0] + zrs[1] + zrs[2]
    ga[zl] = jnp.concatenate([mine24, jnp.zeros((8, Q), f32)], axis=0).astype(bf16)
    sga = sems(3)
    for k in (1, 3, 2):
        send(rc(ga.at[zl], ga.at[zl], sga + k - 1, at(z_=zline(k))))

    for cp in smcp:
        cp.wait_recv()
    sm2[...] = sm[...] + sum(smz[k] for k in range(1, 8))
    sxy = sems(16)

    @pl.loop(1, 16)
    def _(i):
        rc(sm2, smxy.at[i], sxy + i, xy(i)).start()

    head(12, 25)
    hdcp = pltpu.make_async_copy(hd, hd_out, lsem.at[6])
    hdcp.start()

    @pl.loop(1, 16)
    def _(i):
        rc(sm2, smxy.at[i], sxy + i, xy(i)).wait_recv()

    sums = (sm2[...] + sum(smxy[i] for i in range(1, 16))) * (1.0 / D)
    gram_m = gram[...] * (1.0 / D)
    base = {}
    for j in range(1, 4):
        for s in range(j - 1, -1, -1):
            base[j, s] = 4 * len(base)
    c1, c2 = {}, {}
    for n, s in enumerate((3, 2, 1, 0)):
        m1 = sums[2 * n : 2 * n + 1]
        m2 = sums[2 * n + 1 : 2 * n + 2]
        for j in range(s + 1, 4):
            o = base[j, s]
            m1 = m1 - c1[j] * gram_m[o : o + 1] - c2[j] * gram_m[o + 2 : o + 3]
            m2 = m2 - c1[j] * gram_m[o + 1 : o + 2] - c2[j] * gram_m[o + 3 : o + 4]
        c1[s] = rr[s : s + 1, :] * m1
        c2[s] = rr[s : s + 1, :] * m2
    coef = to_cols(pick_rows([c1[s] for s in range(4)] + [c2[s] for s in range(4)], 8))

    for k in range(1, 4):
        src = (zl - k + 4) % 4
        rc(ga.at[zl], ga.at[src], sga + k - 1, at(z_=zline(k))).wait_recv()
    for zz in range(4):
        g0f[R * zz : R * zz + R, :] = ga[zz].astype(f32)[0:R]
    h = g0f[...]
    for s in (3, 2, 1, 0):
        h = h + cs[0:H, 4 + s : 5 + s] * (h * gain(s)) - coef[0:H, s : s + 1] - coef[0:H, 4 + s : 5 + s] * xhs[s]
    g0b[my_tok, :] = h.astype(bf16)
    sc1 = sems(1)
    g0cp = send(rc(g0b.at[my_tok, :], g0b.at[my_tok, :], sc1, at(c_=1 - c)))
    rc(g0b.at[my_tok, :], g0b.at[other_tok, :], sc1, at(c_=1 - c)).wait_recv()
    g0_out[...] = g0b[...]

    for cp in pending:
        cp.wait_send()

    @pl.loop(1, 16)
    def _(i):
        rc(xt, xsl.at[0], s1 + i, xy(i)).wait_send()
        rc(st2.at[mine], st2.at[mine], s3 + i, xy(i)).wait_send()
        rc(sm2, smxy.at[i], sxy + i, xy(i)).wait_send()

    hdcp.wait()


def add_rows(hd, g0, ids, out):
    first = lax.axis_index("tensor") * V + pl.program_id(0) * out.shape[0]
    rows = iota((out.shape[0], T), 0) + first
    onehot = (rows == ids[...]).astype(f32).astype(bf16)
    added = jnp.dot(onehot, g0[...], preferred_element_type=f32).astype(bf16)
    out[...] = (hd[...].astype(f32) + added.astype(f32)).astype(bf16)


def local(emb, final_hidden, section_inputs, gains, token_ids, targets):
    any_ = pl.BlockSpec(memory_space=pl.ANY)
    vm = lambda shape, dtype=f32: pltpu.VMEM(shape, dtype)
    tile = (8, 128)
    hd, g0 = pl.pallas_call(
        kernel,
        out_shape=(jax.ShapeDtypeStruct((V, Q), bf16), jax.ShapeDtypeStruct((T, Q), bf16)),
        in_specs=[any_] * 5,
        out_specs=(any_, pl.BlockSpec(memory_space=pltpu.VMEM)),
        scratch_shapes=[
            vm((W, C), bf16), vm((V, Q), bf16), vm((T, C), bf16), vm((T, C), bf16),
            vm((1, C)), vm((1, T), jnp.int32), vm((T, 1), jnp.int32), vm((8, C)),
            vm((T, W)), vm((3, B, W)), vm((B, W)), vm((B, W)), vm((4, T, W), bf16),
            vm((8,) + tile), vm((16,) + tile), vm((128, 128)),
            vm(tile), vm((16,) + tile), vm((2,) + tile), vm((4, H, Q), bf16), vm((4, 8, Q)),
            vm((128, 128)), vm(tile), vm((4, H, Q)),
            vm((24, 128)), vm((3, 24, 128)), vm((24, 128)), vm((3, 24, 128)),
            vm((24, 128)), vm((24, 128)), vm((24, 128)),
            vm((T, Q)), vm((H, Q)), vm((H, Q)), vm((3, R, Q)), vm((4, 32, Q), bf16),
            vm(tile), vm((8,) + tile), vm(tile), vm((16,) + tile), vm((H, Q)), vm((T, Q), bf16),
            vm((V, Q), bf16),
            pltpu.SemaphoreType.DMA((7,)),
            pltpu.SemaphoreType.DMA((N_SEM,)), pltpu.SemaphoreType.DMA((N_SEM,)),
        ],
        name="relay",
        compiler_params=pltpu.CompilerParams(
            collective_id=0, has_side_effects=True, vmem_limit_bytes=40 * 2**20
        ),
    )(emb, final_hidden, section_inputs, gains, targets.reshape(1, T))
    step = 640
    return pl.pallas_call(
        add_rows,
        grid=(V // step,),
        out_shape=jax.ShapeDtypeStruct((V, Q), bf16),
        in_specs=[
            pl.BlockSpec((step, Q), lambda i: (i, 0)),
            pl.BlockSpec((T, Q), lambda i: (0, 0)),
            pl.BlockSpec((1, T), lambda i: (0, 0)),
        ],
        out_specs=pl.BlockSpec((step, Q), lambda i: (i, 0)),
        name="add_rows",
    )(hd, g0, token_ids.reshape(1, T))


def solution(mesh):
    placed = (P("tensor", "dp"), P(None, "dp"), P("pipe", None, "dp"), P("pipe", "dp"), P(), P())
    return jax.shard_map(
        local, mesh=mesh, in_specs=placed, out_specs=P("tensor", ("dp", "pipe")), check_vma=False
    )
```

time: 545 us -> 79.1 us (0.15)
  waiting for transfers between devices: 255 us -> 0 us
  blocking collectives: 204 us -> 0 us
  Pallas kernels: 0 us -> 69.3 us
  matrix products: 27.1 us -> 0 us
  other arithmetic: 18.9 us -> 0 us
  between operations: 14.1 us -> 0.02 us
  local copies, waits for them, and re-layouts: 20.4 us -> 9.38 us
    psum x6 -> x0, blocking collectives: 182 us -> none  [the longest x5 123 us: feature_sums(): return lax.psum((first, second), 'dp')]
    unnamed x3 -> x0, waiting for transfers between devices: 114 us -> none
    psum x1 -> x0, waiting for transfers between devices: 112 us -> none  [feature_sums(): return lax.psum((first, second), 'dp')]
    pallas_call x0 -> x2, Pallas kernels: none -> 69.3 us  [the longest x1 64 us: local(): pl.pallas_call(kernel, out_shape=(jax.ShapeDtypeStruct((V, Q), bf16), jax...]
    ppermute x3 -> x0, waiting for transfers between devices: 29 us -> none  [passed_along(): lax.ppermute(value, axis, [(source, source + steps) for source in range(l...]
    dot_general x3 -> x0, matrix products: 27.1 us -> none  [the longest x1 11.8 us: local(): lax.dot_general(logit_grad, final_hidden, (((0,), (0,)), ((), ())), prefe...]
    unnamed x1 -> x0, blocking collectives: 22.7 us -> none
    scatter-add x1 -> x0, other arithmetic: 10.9 us -> none  [input_rows(): jax.ops.segment_sum(gradient.astype(jnp.float32), target_rows, vocab_rows...]
  transfers between devices with their start and end apart: 5 -> 0, of which waited for: 5 -> 0; matrix products, arithmetic and copies ran while one was open for 0% -> 0% of each run, Pallas kernels for 0% -> 0%
where the time goes in v1:
time: 79.1 us; the launch traced here: 78.7 us
  Pallas kernels  69.3 us (88%)
  local copies, waits for them, and re-layouts  9.38 us (12%)
    pallas_call x1, Pallas kernels, local(): pl.pallas_call(kernel, out_shape=(jax.ShapeDtypeStruct((V, Q), bf16), jax...  64 us
    unnamed x14, local copies, waits for them, and re-layouts  9.38 us
    pallas_call x1, Pallas kernels, local(): pl.pallas_call(add_rows, grid=(V // step,), out_shape=jax.ShapeDtypeStruc...  5.34 us

profile of v1, /device:TPU:1, one launch (start us, length us, event | category | flops | bytes accessed | tf_op | source)
XLA Modules:
  0.0 78.7 jit_solution(15772856922380218014)
XLA Ops:
  0.0 0.0 copy-start
  0.0 3.8 %copy-done = bf16[3200,1536]{1,0:T(8,128)(2,1)S(1)} copy-done((bf16[3200,1536]{1,0:T(8,128)(2,1)S(1)}, bf16[3200,1536]{1,0:T(8,128)(2,1)}, u32[]{:S(2)}) %copy-start) | copy-done | bytes 9830424
  3.8 0.0 copy-start.2
  3.8 1.1 %copy-done.2 = bf16[192,1536]{1,0:T(8,128)(2,1)S(1)} copy-done((bf16[192,1536]{1,0:T(8,128)(2,1)S(1)}, bf16[192,1536]{1,0:T(8,128)(2,1)}, u32[]{:S(2)}) %copy-start.2) | copy-done | bytes 589848
  4.9 0.0 copy-start.3
  4.9 1.1 %copy-done.3 = bf16[1,192,1536]{2,1,0:T(8,128)(2,1)S(1)} copy-done((bf16[1,192,1536]{2,1,0:T(8,128)(2,1)S(1)}, bf16[1,192,1536]{2,1,0:T(8,128)(2,1)}, u32[]{:S(2)}) %copy-start.3) | copy-done | bytes 589848
  5.9 0.0 copy-start.5
  5.9 0.7 copy-done.5
  6.6 0.0 copy-start.6
  6.6 0.7 copy-done.6
  7.3 64.0 %relay.1 = (bf16[3200,384]{1,0:T(8,128)(2,1)S(1)}, bf16[192,384]{1,0:T(8,128)(2,1)S(1)}) custom-call(bf16[3200,1536]{1,0:T(8,128)(2,1)S(1)} %copy-done, bf16[192,1536]{1,0:T(8,128)(2,1)S(1)} %copy-done.2, bf16[1,192,1536]{2,1,0:T(8,128)(2,1)S(1)} %copy-done.3, f32[1,1536]{1,0:T(1,128)S(1)} %copy-done.5, s32[1,192]{1,0:T(1,128)S(1)} %bitcast.2), custom_call_target="tpu_custom_call" | custom-call | tf_op jit(solution)/shard_map/relay/pallas_call | solution.py:466
  71.3 0.0 copy-start.1
  71.3 1.4 %copy-done.1 = bf16[3200,384]{1,0:T(8,128)(2,1)} copy-done((bf16[3200,384]{1,0:T(8,128)(2,1)}, bf16[3200,384]{1,0:T(8,128)(2,1)S(1)}, u32[]{:S(2)}) %copy-start.1) | copy-done | bytes 2457624
  72.7 0.0 copy-start.4
  72.7 0.6 copy-done.4
  73.4 5.3 %add_rows.1 = bf16[3200,384]{1,0:T(8,128)(2,1)} custom-call(bf16[3200,384]{1,0:T(8,128)(2,1)} %copy-done.1, bf16[192,384]{1,0:T(8,128)(2,1)} %copy-done.4, s32[1,192]{1,0:T(1,128)} %bitcast.3), custom_call_target="tpu_custom_call" | custom-call | tf_op jit(solution)/shard_map/add_rows/pallas_call | solution.py:492
Async XLA Ops:
  0.0 3.8 %copy-start = (bf16[3200,1536]{1,0:T(8,128)(2,1)S(1)}, bf16[3200,1536]{1,0:T(8,128)(2,1)}, u32[]{:S(2)}) copy-start(bf16[3200,1536]{1,0:T(8,128)(2,1)} %emb.1) | copy-start | bytes 29491204
  3.8 1.1 %copy-start.2 = (bf16[192,1536]{1,0:T(8,128)(2,1)S(1)}, bf16[192,1536]{1,0:T(8,128)(2,1)}, u32[]{:S(2)}) copy-start(bf16[192,1536]{1,0:T(8,128)(2,1)} %fh_h.1) | copy-start | bytes 1769476
  4.9 1.1 %copy-start.3 = (bf16[1,192,1536]{2,1,0:T(8,128)(2,1)S(1)}, bf16[1,192,1536]{2,1,0:T(8,128)(2,1)}, u32[]{:S(2)}) copy-start(bf16[1,192,1536]{2,1,0:T(8,128)(2,1)} %x_h.1) | copy-start | bytes 1769476
  5.9 0.7 copy-start.5
  6.6 0.7 copy-start.6
  71.3 1.4 %copy-start.1 = (bf16[3200,384]{1,0:T(8,128)(2,1)}, bf16[3200,384]{1,0:T(8,128)(2,1)S(1)}, u32[]{:S(2)}) copy-start(bf16[3200,384]{1,0:T(8,128)(2,1)S(1)} %get-tuple-element.7.hd) | copy-start | bytes 7372804
  72.7 0.7 copy-start.4

commit v2 on v0

v2 whole, which is shorter than its diff:
```python
import functools

import jax
import jax.numpy as jnp
from jax import lax
from jax.experimental import pallas as pl
from jax.experimental.pallas import tpu as pltpu
from jax.sharding import PartitionSpec as P

eps = 1e-05
f32 = jnp.float32
bf16 = jnp.bfloat16
MESH = pl.DeviceIdType.MESH
LOW = -3.0e38

T, V, C = 192, 3200, 1536
D = 12288
W = 896
Q = 384
B = 48
H = 96
R = 24
N_SEM = 48
CHUNKS = ((0, 512), (512, 384))
STEP = 640


def iota(shape, axis):
    return lax.broadcasted_iota(jnp.int32, shape, axis)


def pick_rows(rows, count):
    index = iota((8, 128), 0)
    tiles = []
    for start in range(0, count, 8):
        out = jnp.zeros((8, 128), f32)
        for i, row in enumerate(rows[start : start + 8]):
            if row is not None:
                out = jnp.where(index == i, jnp.broadcast_to(row, (8, 128)), out)
        tiles.append(out)
    return tiles[0] if len(tiles) == 1 else jnp.concatenate(tiles, axis=0)


def to_rows(cols, count):
    n = cols[0].shape[0]
    lane = iota((n, 128), 1)
    out = jnp.zeros((n, 128), f32)
    for i, col in enumerate(cols):
        out = jnp.where(lane == i, col, out)
    out = jnp.concatenate([out, jnp.zeros((128 - n, 128), f32)], axis=0)
    return out.T[:count]


def rsum(v):
    return jnp.sum(v, axis=1, keepdims=True)


def to_cols(tile):
    r = tile.shape[0]
    if r < 128:
        tile = jnp.concatenate([tile, jnp.zeros((128 - r, 128), f32)], axis=0)
    return tile.T


def kernel(
    emb, fh_h, x_h, gains_h, tgt_h, hd, g0b,
    ew, ec, fh, xv, gv, tv, tcol, gb,
    lp, ly, zl_buf, zr_buf, pb, pn,
    st, st2, sc,
    xt, xsl, xz, xs, gs, cs, rr, xhs,
    gt, gx, gt2, gy, gt3, gz, gram,
    G, cr, gh, zrs, ga, sm, smz, sm2, smxy, g0f, g0s,
    lsem, ss, rs,
):
    d = lax.axis_index("dp")
    px = lax.axis_index("pipe")
    t = lax.axis_index("tensor")
    y, zh = lax.rem(d, 4), lax.div(d, 4)
    zl, c = lax.rem(lax.div(t, 2), 4), lax.rem(t, 2)
    z = zh * 4 + zl
    oc = 1 - c
    xs_at = [lax.rem(px + k, 4) for k in range(4)]
    ys_at = [lax.rem(y + k, 4) for k in range(4)]
    zl_at = [lax.rem(zl + k, 4) for k in range(4)]
    zr_at = [lax.rem(z + k, 8) for k in range(8)]
    base = d - y
    plane = [(base + ys_at[j], xs_at[i], t) for i in range(4) for j in range(4)]
    ring = [(lax.div(zz, 4) * 4 + y, px, lax.rem(zz, 4) * 2 + c) for zz in zr_at]
    group = [(d, px, zl_at[k // 2] * 2 + (oc if k % 2 else c)) for k in range(8)]
    line = [group[2 * k] for k in range(4)]
    twin = group[1]

    used = [0]

    def sems(n):
        used[0] += n
        assert used[0] <= N_SEM
        return used[0] - n

    sent = []

    def send(src, dst, i, dev):
        pltpu.make_async_remote_copy(
            src_ref=src, dst_ref=dst, send_sem=ss.at[i], recv_sem=rs.at[i],
            device_id=dev, device_id_type=MESH,
        ).start()

    def landed(ref, i):
        pltpu.make_async_copy(ref, ref, rs.at[i]).wait()
        sent.append((ref, i))

    def flush():
        for ref, i in sent:
            pltpu.make_async_copy(ref, ref, ss.at[i]).wait()
        sent.clear()

    mult = pl.multiple_of
    my_tok = pl.ds(mult(c * H, 16), H)
    other_tok = pl.ds(mult(oc * H, 16), H)
    my_rows = pl.ds(mult(y * B, 16), B)
    my_cols = pl.ds(mult(px * Q, 128), Q)
    mine = px * 4 + y
    nc = len(CHUNKS)

    bar = pltpu.get_barrier_semaphore()
    copies = [(fh_h, fh)]
    for lo, size in CHUNKS:
        copies.append((emb.at[pl.ds(mult(px * 768 + lo, 128), size), :], ew.at[pl.ds(lo, size), :]))
    copies += [(x_h.at[0], xv), (gains_h, gv), (tgt_h, tv)]
    for i in range(4):
        copies.append((emb.at[pl.ds(768 * i, W), my_cols], ec.at[pl.ds(W * i, W), :]))
    loads = [pltpu.make_async_copy(src, dst, lsem.at[i]) for i, (src, dst) in enumerate(copies)]
    early, late = loads[: 1 + nc], loads[1 + nc :]
    for cp in early:
        cp.start()
    for dev in plane[1:] + ring[1:] + group[1::2]:
        pl.semaphore_signal(bar, inc=1, device_id=dev, device_id_type=MESH)
    for cp in late:
        cp.start()

    loads[0].wait()
    sy = sems(nc)
    for n, (lo, size) in enumerate(CHUNKS):
        lanes = pl.ds(lo, size)
        loads[1 + n].wait()
        lp[:, lanes] = lax.dot_general(
            fh[...], ew[lanes, :], (((1,), (1,)), ((), ())), preferred_element_type=f32
        )
        if n == 0:
            pl.semaphore_wait(bar, 26)
        for k in (1, 3, 2):
            send(lp.at[pl.ds(mult(ys_at[k] * B, 16), B), lanes], ly.at[k - 1, :, lanes], sy + n, plane[k])

    late[0].wait()
    late[1].wait()
    late[2].wait()
    gb[...] = jnp.broadcast_to(gv[...], (8, C))
    sx = sems(2)
    for k in range(1, 4):
        cols = pl.ds(mult(xs_at[k] * Q, 128), Q)
        send(xv.at[my_tok, cols], xs.at[px], sx, plane[4 * k])
        send(gb.at[:, cols], gs.at[px], sx + 1, plane[4 * k])
    xf = xv[my_tok, :].astype(f32)
    xt[...] = to_rows([rsum(xf), rsum(xf * xf)], 8)
    xsl[mine] = xt[...]
    s1 = sems(1)
    for dev in plane[1:]:
        send(xt, xsl.at[mine], s1, dev)
    xs[px] = xv[my_tok, my_cols]
    gs[px] = gb[:, my_cols]
    tcol[...] = rsum(
        jnp.where(iota((T, T), 0) == iota((T, T), 1), tv[...].astype(f32), 0.0)
    ).astype(jnp.int32)

    sz = sems(nc)
    for n, (lo, size) in enumerate(CHUNKS):
        lanes = pl.ds(lo, size)
        landed(ly.at[:, :, lanes], sy + n)
        zl_buf[:, lanes] = lp[my_rows, lanes] + ly[0, :, lanes] + ly[1, :, lanes] + ly[2, :, lanes]
        send(zl_buf.at[:, lanes], zr_buf.at[:, lanes], sz + n, ring[4])

    landed(xsl.at[pl.ds(0, 15)], s1)
    rows = []
    for s in range(4):
        tot = xsl[4 * s] + xsl[4 * s + 1] + xsl[4 * s + 2] + xsl[4 * s + 3]
        rows += [tot[0:1], tot[1:2]]
    xz[0] = pick_rows(rows, 8)
    s2 = sems(1)
    send(xz.at[0], xz.at[1], s2, ring[4])
    landed(xs.at[pl.ds(0, 3)], sx)
    landed(gs.at[pl.ds(0, 3)], sx + 1)
    landed(xz.at[1], s2)
    tot = (xz[0] + xz[1]) * (1.0 / D)
    mu_rows, r_rows = [], []
    for s in range(4):
        mu = tot[2 * s : 2 * s + 1]
        mu_rows.append(mu)
        r_rows.append(lax.rsqrt(tot[2 * s + 1 : 2 * s + 2] - mu * mu + eps))
    rr[...] = pick_rows(r_rows, 8)
    cs[...] = to_cols(pick_rows(mu_rows + r_rows, 8))
    for s in range(4):
        xhs[s] = (xs[s].astype(f32) - cs[0:H, s : s + 1]) * cs[0:H, 4 + s : 5 + s]

    def gain(s):
        return gs[s][0:1, :]

    cols = []
    for j in range(1, 4):
        q1 = jnp.ones((H, Q), f32)
        q2 = xhs[j]
        for s in range(j - 1, -1, -1):
            a1 = q1 * gain(s)
            a2 = q2 * gain(s)
            xh = xhs[s]
            cols += [rsum(a1), rsum(a1 * xh), rsum(a2), rsum(a2 * xh)]
            if s > 0:
                r_col = cs[0:H, 4 + s : 5 + s]
                q1 = q1 + r_col * a1
                q2 = q2 + r_col * a2
    gt[...] = to_rows(cols, 24)
    sgx = sems(1)
    for k in range(1, 4):
        send(gt, gx.at[k - 1], sgx, plane[4 * k])

    first = [(base + lax.rem(y + k * oc, 4), lax.rem(px + k * c, 4), t) for k in range(4)]
    second = [(base + lax.rem(y + k * c, 4), lax.rem(px + k * oc, 4), t) for k in range(4)]

    def block(b, e_):
        return lax.rem(px - b * c - e_ * oc + 4, 4), lax.rem(y - b * oc - e_ * c + 4, 4)

    def pref(n, b):
        bx, by = block(b, 0)
        lo, size = CHUNKS[n]
        return pb.at[bx, pl.ds(mult(by * B, 16), B), pl.ds(lo, size)]

    a1 = sems(3 * nc)
    a2 = sems(4 * nc)

    def first_sends(n):
        own = pref(n, 0)
        for k in (1, 3, 2):
            send(own, own, a1 + 3 * n + k - 1, first[k])

    def second_sends(n, b):
        own = pref(n, b)
        for k in (1, 3, 2):
            send(own, own, a2 + 4 * n + b, second[k])

    def forward(n):
        for b in (1, 3, 2):
            landed(pref(n, b), a1 + 3 * n + b - 1)
            second_sends(n, b)

    first_lane = jnp.where(px == 0, 0, 128)
    tops, sums_, hits = [], [], []
    for n, (lo, size) in enumerate(CHUNKS):
        lanes = pl.ds(lo, size)
        landed(zr_buf.at[:, lanes], sz + n)
        lane = iota((B, size), 1) + lo
        valid = lane >= first_lane
        logits = jnp.where(valid, zl_buf[:, lanes] + zr_buf[:, lanes], LOW)
        m = jnp.max(logits, axis=1, keepdims=True)
        e = jnp.where(valid, jnp.exp(logits - m), 0.0)
        hit = (lane + (t * V + px * 768) == tcol[my_rows, :]) & valid
        pb[px, my_rows, lanes] = e.astype(bf16)
        first_sends(n)
        second_sends(n, 0)
        tops.append(m)
        sums_.append(rsum(e))
        hits.append(rsum(jnp.where(hit, logits, 0.0)))
        if n:
            forward(n - 1)

    top = functools.reduce(jnp.maximum, tops)
    total = sum(a * jnp.exp(b - top) for a, b in zip(sums_, tops))
    st[0] = to_rows([top, total, sum(hits)] + tops, 8)
    sst = sems(1)
    for k in range(1, 8):
        send(st.at[0], st.at[k], sst, group[k])

    landed(gx, sgx)
    gt2[...] = gt[...] + gx[0] + gx[1] + gx[2]
    sgy = sems(1)
    for k in range(1, 4):
        send(gt2, gy.at[k - 1], sgy, plane[k])

    forward(nc - 1)

    landed(st.at[pl.ds(1, 7)], sst)
    tiles = [st[k] for k in range(8)]
    top = functools.reduce(jnp.maximum, [a[0:1] for a in tiles])
    total = sum(a[1:2] * jnp.exp(a[0:1] - top) for a in tiles)
    st2[mine] = pick_rows(
        [top, total, sum(a[2:3] for a in tiles)] + [tiles[0][3 + n : 4 + n] for n in range(len(CHUNKS))], 8
    )
    s3 = sems(1)
    for dev in plane[1:]:
        send(st2.at[mine], st2.at[mine], s3, dev)

    landed(gy, sgy)
    gt3[...] = gt2[...] + gy[0] + gy[1] + gy[2]
    sgz = sems(1)
    send(gt3, gz, sgz, ring[4])
    landed(st2.at[pl.ds(0, 15)], s3)

    rows = []
    for yy in range(4):
        tiles = [st2[4 * xx + yy] for xx in range(4)]
        top = functools.reduce(jnp.maximum, [a[0:1] for a in tiles])
        total = sum(a[1:2] * jnp.exp(a[0:1] - top) for a in tiles)
        inv = 1.0 / total
        rows += [jnp.exp(a[3 + n : 4 + n] - top) * inv for a in tiles for n in range(4)]
        rows += [jnp.exp(sum(a[2:3] for a in tiles) - top) * inv - 1.0]
        rows += [None] * 15
    sc[...] = to_cols(pick_rows(rows, 128))

    def normalise(n, b, e_):
        bx, by = block(b, e_)
        lo, size = CHUNKS[n]
        lanes = pl.ds(lo, size)
        blk = pl.ds(mult(by * B, 16), B)
        pick = iota((B, 128), 1)
        scale = rsum(jnp.where(pick == by * 32 + bx * 4 + n, sc[0:B, :], 0.0))
        point = rsum(jnp.where(pick == by * 32 + 16, sc[0:B, :], 0.0))
        lane = iota((B, size), 1) + lo
        hit = (lane + (t * V + bx * 768) == tcol[blk, :]) & (lane >= jnp.where(bx == 0, 0, 128))
        pn[blk, pl.ds(mult(bx * W + lo, 128), size)] = jnp.where(hit, point, pb[bx, blk, lanes].astype(f32) * scale).astype(bf16)

    for n, (lo, size) in enumerate(CHUNKS):
        @pl.loop(0, 4)
        def _(b):
            normalise(n, b, 0)

        for b in (0, 1, 3, 2):
            landed(pb.at[0, pl.ds(0, 3 * B), pl.ds(lo, size)], a2 + 4 * n + b)

            @pl.loop(1, 4)
            def _(k):
                normalise(n, b, k)

    for cp in late[3:]:
        cp.wait()
    G[...] = jnp.dot(pn[...], ec[...], preferred_element_type=f32)

    sc0 = sems(1)
    send(G.at[other_tok, :], cr, sc0, twin)
    landed(gz, sgz)
    gram[...] = gt3[...] + gz[...]
    landed(cr, sc0)
    gh[...] = G[my_tok, :] + cr[...]
    szr = sems(1)
    for k in (1, 3, 2):
        send(gh.at[pl.ds(mult(zl_at[k] * R, 8), R), :], zrs.at[k - 1], szr, line[k])

    q = gh[...]
    cols = []
    for s in (3, 2, 1, 0):
        a = q * gain(s)
        cols += [rsum(a), rsum(a * xhs[s])]
        if s > 0:
            q = q + cs[0:H, 4 + s : 5 + s] * a
    sm[...] = to_rows(cols, 8)
    ssm = sems(1)
    for k in range(1, 8):
        send(sm, smz.at[k], ssm, ring[k])

    fcols = fh[:, my_cols]

    def head(windows):
        for i in windows:
            lo = 128 if i else 0
            res = lax.dot_general(
                pn[:, W * i + lo : W * (i + 1)], fcols, (((0,), (0,)), ((), ())), preferred_element_type=f32
            )
            hd[768 * i + lo : 768 * i + W, :] = res.astype(bf16)

    head((0,))
    landed(zrs, szr)
    mine24 = gh[pl.ds(mult(zl * R, 8), R), :] + zrs[0] + zrs[1] + zrs[2]
    ga[zl] = jnp.concatenate([mine24, jnp.zeros((8, Q), f32)], axis=0).astype(bf16)
    sga = sems(1)
    for k in (1, 3, 2):
        send(ga.at[zl], ga.at[zl], sga, line[k])

    landed(smz.at[pl.ds(1, 7)], ssm)
    sm2[...] = sm[...] + sum(smz[k] for k in range(1, 8))
    sxy = sems(1)
    for i in range(1, 16):
        send(sm2, smxy.at[i], sxy, plane[i])

    flush()
    head((1, 2, 3))
    landed(smxy.at[pl.ds(1, 15)], sxy)

    sums = (sm2[...] + sum(smxy[i] for i in range(1, 16))) * (1.0 / D)
    gram_m = gram[...] * (1.0 / D)
    at = {}
    for j in range(1, 4):
        for s in range(j - 1, -1, -1):
            at[j, s] = 4 * len(at)
    c1, c2 = {}, {}
    for n, s in enumerate((3, 2, 1, 0)):
        m1 = sums[2 * n : 2 * n + 1]
        m2 = sums[2 * n + 1 : 2 * n + 2]
        for j in range(s + 1, 4):
            o = at[j, s]
            m1 = m1 - c1[j] * gram_m[o : o + 1] - c2[j] * gram_m[o + 2 : o + 3]
            m2 = m2 - c1[j] * gram_m[o + 1 : o + 2] - c2[j] * gram_m[o + 3 : o + 4]
        c1[s] = rr[s : s + 1, :] * m1
        c2[s] = rr[s : s + 1, :] * m2
    coef = to_cols(pick_rows([c1[s] for s in range(4)] + [c2[s] for s in range(4)], 8))

    landed(ga.at[pl.ds(0, 3)], sga)
    for zz in range(4):
        g0f[R * zz : R * zz + R, :] = ga[zz].astype(f32)[0:R]
    h = g0f[...]
    for s in (3, 2, 1, 0):
        h = h + cs[0:H, 4 + s : 5 + s] * (h * gain(s)) - coef[0:H, s : s + 1] - coef[0:H, 4 + s : 5 + s] * xhs[s]
    g0s[my_tok, :] = h.astype(bf16)
    sc1 = sems(1)
    send(g0s.at[my_tok, :], g0s.at[my_tok, :], sc1, twin)
    landed(g0s.at[other_tok, :], sc1)
    g0b[...] = g0s[...]
    flush()


def add_rows(hd, g0, ids, out, res, osem):
    parts = [pl.ds(i * STEP, STEP) for i in range(V // STEP)]
    first = lax.axis_index("tensor") * V
    stores = []
    for i, p in enumerate(parts):
        rows = iota((STEP, T), 0) + (first + i * STEP)
        onehot = jnp.where(rows == ids[...], 1.0, 0.0).astype(bf16)
        added = jnp.dot(onehot, g0[...], preferred_element_type=f32).astype(bf16)
        res[p, :] = (hd[p, :].astype(f32) + added.astype(f32)).astype(bf16)
        stores.append(pltpu.make_async_copy(res.at[p, :], out.at[p, :], osem.at[i]))
        stores[-1].start()
    for cp in stores:
        cp.wait()


def local(emb, final_hidden, section_inputs, gains, token_ids, targets):
    hbm = pl.BlockSpec(memory_space=pltpu.HBM)
    vmem = pl.BlockSpec(memory_space=pltpu.VMEM)
    vm = lambda shape, dtype=f32: pltpu.VMEM(shape, dtype)
    tile = (8, 128)
    args = (emb, final_hidden, section_inputs, gains, targets.reshape(1, T))
    hd, g0 = pl.pallas_call(
        kernel,
        out_shape=(pltpu.VMEM((V, Q), bf16), pltpu.VMEM((T, Q), bf16)),
        in_specs=[hbm] * 5,
        out_specs=(vmem, vmem),
        scratch_shapes=[
            vm((W, C), bf16), vm((4 * W, Q), bf16), vm((T, C), bf16), vm((T, C), bf16),
            vm((1, C)), vm((1, T), jnp.int32), vm((T, 1), jnp.int32), vm((8, C)),
            vm((T, W)), vm((3, B, W)), vm((B, W)), vm((B, W)), vm((4, T, W), bf16), vm((T, 4 * W), bf16),
            vm((8,) + tile), vm((16,) + tile), vm((128, 128)),
            vm(tile), vm((16,) + tile), vm((2,) + tile), vm((4, H, Q), bf16), vm((4, 8, Q)),
            vm((128, 128)), vm(tile), vm((4, H, Q)),
            vm((24, 128)), vm((3, 24, 128)), vm((24, 128)), vm((3, 24, 128)),
            vm((24, 128)), vm((24, 128)), vm((24, 128)),
            vm((T, Q)), vm((H, Q)), vm((H, Q)), vm((3, R, Q)), vm((4, 32, Q), bf16),
            vm(tile), vm((8,) + tile), vm(tile), vm((16,) + tile), vm((H, Q)), vm((T, Q), bf16),
            pltpu.SemaphoreType.DMA((12,)),
            pltpu.SemaphoreType.DMA((N_SEM,)), pltpu.SemaphoreType.DMA((N_SEM,)),
        ],
        name="relay",
        compiler_params=pltpu.CompilerParams(
            collective_id=0, has_side_effects=True, vmem_limit_bytes=40 * 2**20
        ),
    )(*[pltpu.with_memory_space_constraint(a, pltpu.HBM) for a in args])
    return pl.pallas_call(
        add_rows,
        out_shape=jax.ShapeDtypeStruct((V, Q), bf16),
        in_specs=[vmem] * 3,
        out_specs=pl.BlockSpec(memory_space=pl.ANY),
        scratch_shapes=[vm((V, Q), bf16), pltpu.SemaphoreType.DMA((V // STEP,))],
        name="add_rows",
        compiler_params=pltpu.CompilerParams(vmem_limit_bytes=30 * 2**20),
    )(
        pltpu.with_memory_space_constraint(hd, pltpu.VMEM),
        pltpu.with_memory_space_constraint(g0, pltpu.VMEM),
        token_ids.reshape(1, T),
    )


def solution(mesh):
    placed = (P("tensor", "dp"), P(None, "dp"), P("pipe", None, "dp"), P("pipe", "dp"), P(), P())
    return jax.shard_map(
        local, mesh=mesh, in_specs=placed, out_specs=P("tensor", ("dp", "pipe")), check_vma=False
    )
```

time: 545 us -> 66.6 us (0.12)
  waiting for transfers between devices: 255 us -> 0 us
  blocking collectives: 204 us -> 0 us
  Pallas kernels: 0 us -> 66.6 us
  matrix products: 27.1 us -> 0 us
  local copies, waits for them, and re-layouts: 20.4 us -> 0.01 us
  other arithmetic: 18.9 us -> 0 us
  between operations: 14.1 us -> 0.02 us
    psum x6 -> x0, blocking collectives: 182 us -> none  [the longest x5 123 us: feature_sums(): return lax.psum((first, second), 'dp')]
    unnamed x3 -> x0, waiting for transfers between devices: 114 us -> none
    psum x1 -> x0, waiting for transfers between devices: 112 us -> none  [feature_sums(): return lax.psum((first, second), 'dp')]
    pallas_call x0 -> x2, Pallas kernels: none -> 66.6 us  [the longest x1 64.6 us: local(): pl.pallas_call(kernel, out_shape=(pltpu.VMEM((V, Q), bf16), pltpu.VMEM((T...]
    ppermute x3 -> x0, waiting for transfers between devices: 29 us -> none  [passed_along(): lax.ppermute(value, axis, [(source, source + steps) for source in range(l...]
    dot_general x3 -> x0, matrix products: 27.1 us -> none  [the longest x1 11.8 us: local(): lax.dot_general(logit_grad, final_hidden, (((0,), (0,)), ((), ())), prefe...]
    unnamed x1 -> x0, blocking collectives: 22.7 us -> none
    unnamed x19 -> x2, local copies, waits for them, and re-layouts: 20.1 us -> 0.01 us
  transfers between devices with their start and end apart: 5 -> 0, of which waited for: 5 -> 0; matrix products, arithmetic and copies ran while one was open for 0% -> 0% of each run, Pallas kernels for 0% -> 0%
where the time goes in v2:
time: 66.6 us
  Pallas kernels  66.6 us (100%)
    pallas_call x1, Pallas kernels, local(): pl.pallas_call(kernel, out_shape=(pltpu.VMEM((V, Q), bf16), pltpu.VMEM((T...  64.6 us
    pallas_call x1, Pallas kernels, local(): pl.pallas_call(add_rows, out_shape=jax.ShapeDtypeStruct((V, Q), bf16), in...  1.91 us

profile of v2, /device:TPU:1, one launch (start us, length us, event | category | flops | bytes accessed | tf_op | source)
XLA Modules:
  0.0 66.6 jit_solution(12922560636014369350)
XLA Ops:
  0.0 0.0 copy-start
  0.0 64.6 %relay.1 = (bf16[3200,384]{1,0:T(8,128)(2,1)S(1)}, bf16[192,384]{1,0:T(8,128)(2,1)S(1)}) custom-call(bf16[3200,1536]{1,0:T(8,128)(2,1)} %emb.1, bf16[192,1536]{1,0:T(8,128)(2,1)} %fh_h.1, bf16[1,192,1536]{2,1,0:T(8,128)(2,1)} %x_h.1, f32[1,1536]{1,0:T(1,128)} %gains_h.1, s32[1,192]{1,0:T(1,128)} %bitcast.3), custom_call_target="tpu_custom_call" | custom-call | tf_op jit(solution)/shard_map/relay/pallas_call | solution.py:448
  64.7 0.0 copy-done
  64.7 1.9 %add_rows.1 = bf16[3200,384]{1,0:T(8,128)(2,1)} custom-call(bf16[3200,384]{1,0:T(8,128)(2,1)S(1)} %get-tuple-element.7.hd, bf16[192,384]{1,0:T(8,128)(2,1)S(1)} %get-tuple-element.8.g0, s32[1,192]{1,0:T(1,128)S(1)} %bitcast.2), custom_call_target="tpu_custom_call" | custom-call | tf_op jit(solution)/shard_map/add_rows/pallas_call | solution.py:472
Async XLA Ops:
  0.0 64.7 %copy-start = (s32[192]{0:T(256)S(1)}, s32[192]{0:T(256)}, u32[]{:S(2)}) copy-start(s32[192]{0:T(256)} %param.10) | copy-start | bytes 2308
